TPU v7x, 256 devices: a whole 4x4x8 slice. The times are simulated.
256 devices in a mesh: wide: 16 (over y, z_lo), narrow: 16 (over x, z_hi, core).
Axes of the slice: x: 4, y: 4, z: 8 (z_hi: 2, z_lo: 4; z = z_hi * 4 + z_lo), core: 2. Of those that a mesh axis runs over, the one named last changes fastest.
Arguments:
- residual: float32 [16, 16, 6, 192, 512], P('wide', 'narrow'), may hold values from -6 to 6
- face_schur: float32 [16, 16, 6, 192, 192], P('wide', 'narrow'), may hold values from -0.5 to 1.5, as said below
- local_solver: bfloat16 [16, 16, 1152, 1152], P('wide', 'narrow'), may hold values from -0.1875 to 0.1875
- interface_functional_set: float32 [3, 192, 16], replicated, may hold values from -0.4375 to 0.4375
- coarse_inverse: float32 [12288, 12288], P('wide', 'narrow'), may hold values from -0.109375 to 0.109375
Outputs:
- preconditioned: float32 [16, 16, 3, 192, 512], P('wide', 'narrow')
Inputs may be any that keep to these rules, and one draw needn't show every extreme that they name: `face_schur`: every face block is symmetric positive definite.
All inputs are finite; a program needn't handle non-finite values. Where the computation divides by a largest or mean magnitude, that divisor is 1e-20 or more.
Results may differ from a plain program's by a relative error of at most 0.002.
Values sent between devices are 32-bit elements; how exact they have to be, the bound alone decides.
A program may use at most 64 MiB of HBM per device.

v0:
```python
import jax
import jax.numpy as jnp
from jax import lax
from jax.sharding import PartitionSpec as P

NS_STEPS = 12
exact_arithmetic_mode = lax.Precision.HIGHEST


def extended(block, sides, width):
    for axis, dim in sides:
        count = lax.axis_size(axis)
        forward = [(i, i + 1) for i in range(count - 1)]
        forward.append((count - 1, 0))
        backward = [(target, source) for source, target in forward]
        low = lax.ppermute(
            lax.slice_in_dim(block, block.shape[dim] - width, None, axis=dim), axis, forward
        )
        high = lax.ppermute(lax.slice_in_dim(block, 0, width, axis=dim), axis, backward)
        block = jnp.concatenate([low, block, high], axis=dim)
    return block


def passed_along(value, axis, steps):
    count = lax.axis_size(axis)
    pairs = [(source, (source + steps) % count) for source in range(count)]
    return lax.ppermute(value, axis, pairs)


def newton_schulz(matrices):
    row_sums = jnp.max(jnp.sum(jnp.abs(matrices), axis=2), axis=1)
    approx = matrices / (row_sums * row_sums)[:, None, None]
    for iteration in range(NS_STEPS):
        product = jnp.einsum("bij,bjk->bik", matrices, approx, precision=exact_arithmetic_mode)
        approx = 2.0 * approx - jnp.einsum(
            "bij,bjk->bik", approx, product, precision=exact_arithmetic_mode
        )
    return approx


def apply_faces(blocks, fields):
    return jnp.einsum("fij,fjr->fir", blocks, fields, precision=exact_arithmetic_mode)


def per_device(residual, face_schur, local_solver, interface_functional_set, coarse_inverse):
    blocks = face_schur[0, 0]
    face_loads = residual[0, 0]
    face_order = blocks.shape[1]
    columns_count = face_loads.shape[2]
    wide_joined = jnp.concatenate([blocks[0:2], face_loads[0:2]], axis=2)
    wide_padded = extended(wide_joined, (("wide", 0),), 1)
    narrow_joined = jnp.concatenate([blocks[2:4], face_loads[2:4]], axis=2)
    slim_side_extended = extended(narrow_joined, (("narrow", 0),), 1)
    face_sums = jnp.stack(
        [
            wide_padded[0, :, :face_order] + blocks[0],
            blocks[1] + wide_padded[3, :, :face_order],
            slim_side_extended[0, :, :face_order] + blocks[2],
            blocks[3] + slim_side_extended[3, :, :face_order],
            blocks[4] + blocks[5],
        ],
        axis=0,
    )
    assembled_vector = jnp.stack(
        [
            wide_padded[0, :, face_order:] + face_loads[0],
            face_loads[1] + wide_padded[3, :, face_order:],
            slim_side_extended[0, :, face_order:] + face_loads[2],
            face_loads[3] + slim_side_extended[3, :, face_order:],
            face_loads[4] + face_loads[5],
        ],
        axis=0,
    )
    owned_values = jnp.stack(
        [assembled_vector[1], assembled_vector[3], assembled_vector[4]], axis=0
    )
    inverse = newton_schulz(face_sums)
    scaled = apply_faces(inverse, assembled_vector)
    face_scaled = jnp.concatenate([scaled, scaled[4:5]], axis=0)
    owned_inverse = jnp.stack([inverse[1], inverse[3], inverse[4]], axis=0)
    restricted_residual = jnp.einsum(
        "psk,pse->pke", interface_functional_set, owned_values, precision=exact_arithmetic_mode
    )
    restricted_residual = restricted_residual.reshape(-1, columns_count)
    incomplete_total = jnp.dot(
        coarse_inverse,
        lax.all_gather(restricted_residual, "wide", axis=0, tiled=True),
        precision=exact_arithmetic_mode,
        preferred_element_type=jnp.float32,
    )
    own_rows = restricted_residual.shape[0]
    summed = lax.psum(incomplete_total, "narrow")
    own_coarse = lax.dynamic_slice_in_dim(summed, lax.axis_index("narrow") * own_rows, own_rows, 0)
    local_loads = apply_faces(blocks, face_scaled).astype(jnp.bfloat16)
    flattened = local_loads.reshape(-1, columns_count)
    solved = jnp.dot(local_solver[0, 0], flattened, preferred_element_type=jnp.float32)
    solved = solved.reshape(6, face_order, columns_count)
    weighted = apply_faces(blocks, solved)
    wide_back = passed_along(weighted[0], "wide", -1)
    narrow_back = passed_along(weighted[2], "narrow", -1)
    combined = jnp.stack(
        [weighted[1] + wide_back, weighted[3] + narrow_back, weighted[4] + weighted[5]], axis=0
    )
    local_part = apply_faces(owned_inverse, combined)
    update_increment = own_coarse.reshape(3, -1, columns_count)
    coarse_component = jnp.einsum(
        "fek,fkg->feg", interface_functional_set, update_increment, precision=exact_arithmetic_mode
    )
    output_answer = local_part + coarse_component
    return output_answer[None, None]


def solution(mesh):
    placed = (
        P("wide", "narrow", None, None, None),
        P("wide", "narrow", None, None, None),
        P("wide", "narrow", None, None),
        P(),
        P("wide", "narrow"),
    )
    return jax.shard_map(
        per_device,
        mesh=mesh,
        in_specs=placed,
        out_specs=P("wide", "narrow", None, None, None),
        check_vma=False,
    )
```

profile of v0, /device:TPU:8, one launch (start us, length us, event | category | flops | bytes accessed | tf_op | source)
XLA Modules:
  0.0 398.9 jit_solution(18344340595628974362)
XLA Ops:
  6.5 1.6 slice_bitcast_fusion
  8.8 2.0 collective-permute-start
  10.8 2.8 collective-permute-start.1
  14.0 8.9 %collective-permute-start.3 = (f32[1,192,704]{2,1,0:T(8,128)S(1)}, f32[1,192,704]{2,1,0:T(8,128)S(1)}, u32[]{:S(2)}, u32[]{:S(2)}) collective-permute-start(f32[1,192,704]{2,1,0:T(8,128)S(1)} %get-tuple-element.18), channel_id=1, source_target_pairs={{1,0},{2,1},{3,2},{4,3},{5,4},{6,5},{7,6},{8,7},{9,8},{10,9},{11,1... | collective-permute-start | bytes 1622024 | tf_op jit(solution)/shard_map/ppermute | solution.py:19
  22.9 5.0 %collective-permute-done = f32[1,192,704]{2,1,0:T(8,128)S(1)} collective-permute-done((f32[1,192,704]{2,1,0:T(8,128)S(1)}, f32[1,192,704]{2,1,0:T(8,128)S(1)}, u32[]{:S(2)}, u32[]{:S(2)}) %collective-permute-start) | collective-permute-done | bytes 540704 | tf_op jit(solution)/shard_map/ppermute | solution.py:16
  27.9 12.8 %collective-permute-done.1 = f32[1,192,704]{2,1,0:T(8,128)S(1)} collective-permute-done((f32[1,192,704]{2,1,0:T(8,128)S(1)}, f32[1,192,704]{2,1,0:T(8,128)S(1)}, u32[]{:S(2)}, u32[]{:S(2)}) %collective-permute-start.1) | collective-permute-done | bytes 540704 | tf_op jit(solution)/shard_map/ppermute | solution.py:19
  40.7 17.0 %collective-permute-done.2 = f32[1,192,704]{2,1,0:T(8,128)S(1)} collective-permute-done((f32[1,192,704]{2,1,0:T(8,128)S(1)}, f32[1,192,704]{2,1,0:T(8,128)S(1)}, u32[]{:S(2)}, u32[]{:S(2)}) %collective-permute-start.2) | collective-permute-done | bytes 540704 | tf_op jit(solution)/shard_map/ppermute | solution.py:16
  60.1 2.8 fusion.22
  62.9 1.2 convolution_subtract_fusion.11
  64.1 1.1 fusion.45
  65.2 1.1 convolution_subtract_fusion.10
  66.3 1.1 fusion.46
  67.4 1.1 convolution_subtract_fusion.9
  68.5 1.1 fusion.47
  69.6 1.1 convolution_subtract_fusion.8
  70.7 1.1 fusion.48
  71.8 1.1 convolution_subtract_fusion.7
  73.0 1.3 fusion.49
  74.2 1.1 convolution_subtract_fusion.6
  75.4 1.1 fusion.50
  76.5 1.1 convolution_subtract_fusion.5
  77.6 1.1 fusion.51
  78.7 2.1 convolution_subtract_fusion.4
  82.3 1.3 copy-done.10
  83.6 1.4 fusion.14
  85.2 2.7 fusion.52
  87.9 1.1 convolution_subtract_fusion.3
  90.2 1.1 convolution_subtract_fusion.2
  91.3 1.1 fusion.54
  92.4 1.1 convolution_subtract_fusion.1
  93.5 1.1 fusion.55
  94.6 1.1 convolution_subtract_fusion
  96.2 1.8 fusion.56
  98.1 3.8 fusion.5
  101.8 70.4 %all-gather.2.cloned.1.call-done = f32[768,512]{1,0:T(8,128)} async-done(((f32[48,512]{1,0:T(8,128)}), f32[768,512]{1,0:T(8,128)}) %all-gather.2.cloned.1.call-update) | async-done | bytes 1572880 | tf_op jit(solution)/shard_map/all_gather | solution.py:87
  172.2 10.8 %convolution_bitcast_fusion.2 = f32[768,512]{0,1:T(8,128)} fusion(f32[768,512]{1,0:T(8,128)} %all-gather.2.cloned.1.call-done, f32[768,768]{1,0:T(8,128)} %param.9), kind=kOutput, calls=%fused_computation.8 | convolution fusion | flops 3623878656 | bytes 5505024 | tf_op jit(solution)/shard_map/dot_general | solution.py:85
  183.1 4.6 %convolution_bitcast_fusion = f32[1152,512]{0,1:T(8,128)} fusion(bf16[1152,512]{1,0:T(8,128)(2,1)} %bitcast.133, bf16[1,1,1152,1152]{3,2,1,0:T(8,128)(2,1)S(1)} %copy-done), kind=kOutput, calls=%fused_computation | convolution fusion | flops 1358954496 | bytes 6193152 | tf_op jit(solution)/shard_map/dot_general | solution.py:96
  187.6 3.2 copy.9
  190.8 4.3 %convolution_bitcast_fusion.1 = f32[6,192,512]{2,1,0:T(8,128)S(1)} fusion(f32[6,192,512]{2,1,0:T(8,128)} %bitcast.132, f32[1,1,6,192,192]{4,3,2,1,0:T(8,128)} %param.6), kind=kOutput, calls=%fused_computation.6 | convolution fusion | flops 1358954496 | bytes 5603328 | tf_op jit(solution)/shard_map/fij,fjr->fir/dot_general | solution.py:42
  195.2 1.4 copy-done.6
  197.6 5.3 %collective-permute-start.4 = (f32[192,512]{1,0:T(8,128)}, f32[192,512]{1,0:T(8,128)}, u32[]{:S(2)}, u32[]{:S(2)}) collective-permute-start(f32[192,512]{1,0:T(8,128)} %get-tuple-element.13), channel_id=1, source_target_pairs={{0,240},{16,0},{32,16},{48,32},{64,48},{80,64},{96,80},{112,96},{1... | collective-permute-start | bytes 1179656 | tf_op jit(solution)/shard_map/ppermute | solution.py:27
  203.0 11.3 %collective-permute-done.4 = f32[192,512]{1,0:T(8,128)} collective-permute-done((f32[192,512]{1,0:T(8,128)}, f32[192,512]{1,0:T(8,128)}, u32[]{:S(2)}, u32[]{:S(2)}) %collective-permute-start.4) | collective-permute-done | bytes 393248 | tf_op jit(solution)/shard_map/ppermute | solution.py:27
  214.2 5.8 %collective-permute-done.5 = f32[192,512]{1,0:T(8,128)} collective-permute-done((f32[192,512]{1,0:T(8,128)}, f32[192,512]{1,0:T(8,128)}, u32[]{:S(2)}, u32[]{:S(2)}) %collective-permute-start.5) | collective-permute-done | bytes 393248 | tf_op jit(solution)/shard_map/ppermute | solution.py:27
  220.0 2.4 fusion.35
  222.4 162.1 %all-reduce.2.cloned.1.call-done = f32[768,512]{0,1:T(8,128)} async-done(((f32[768,512]{0,1:T(8,128)}), f32[768,512]{0,1:T(8,128)}) %all-reduce.2.cloned.1.call-update) | async-done | bytes 1572880 | tf_op jit(solution)/shard_map/psum | solution.py:92
  384.5 1.2 constant_dynamic-slice_fusion
  386.4 2.0 convolution_bitcast_fusion.3
  388.4 3.5 fusion.8
  (67 shorter events, 8.6 us)
Async XLA Ops:
  6.5 176.5 %copy-start = (bf16[1,1,1152,1152]{3,2,1,0:T(8,128)(2,1)S(1)}, bf16[1,1,1152,1152]{3,2,1,0:T(8,128)(2,1)}, u32[]{:S(2)}) copy-start(bf16[1,1,1152,1152]{3,2,1,0:T(8,128)(2,1)} %param.7) | copy-start | bytes 7962628
  6.5 165.7 %all-gather.2.cloned.1.call-start = ((), (), s32[]{:S(2)}) async-start(), calls=%async_computation | async-start | bytes 1671168 | tf_op jit(solution)/shard_map/all_gather | solution.py:87
  6.5 1.9 copy-start.4
  8.8 19.0 %collective-permute-start = (f32[1,192,704]{2,1,0:T(8,128)S(1)}, f32[1,192,704]{2,1,0:T(8,128)S(1)}, u32[]{:S(2)}, u32[]{:S(2)}) collective-permute-start(f32[1,192,704]{2,1,0:T(8,128)S(1)} %get-tuple-element.23), channel_id=1, source_target_pairs={{0,16},{16,32},{32,48},{48,64},{64,80},{80,96},{96,112},{112,128},... | collective-permute-start | bytes 1622024 | tf_op jit(solution)/shard_map/ppermute | solution.py:16
  10.8 29.9 %collective-permute-start.1 = (f32[1,192,704]{2,1,0:T(8,128)S(1)}, f32[1,192,704]{2,1,0:T(8,128)S(1)}, u32[]{:S(2)}, u32[]{:S(2)}) collective-permute-start(f32[1,192,704]{2,1,0:T(8,128)S(1)} %get-tuple-element.22), channel_id=1, source_target_pairs={{16,0},{32,16},{48,32},{64,48},{80,64},{96,80},{112,96},{128,112},... | collective-permute-start | bytes 1622024 | tf_op jit(solution)/shard_map/ppermute | solution.py:19
  13.9 43.8 %collective-permute-start.2 = (f32[1,192,704]{2,1,0:T(8,128)S(1)}, f32[1,192,704]{2,1,0:T(8,128)S(1)}, u32[]{:S(2)}, u32[]{:S(2)}) collective-permute-start(f32[1,192,704]{2,1,0:T(8,128)S(1)} %get-tuple-element.19), channel_id=1, source_target_pairs={{0,1},{1,2},{2,3},{3,4},{4,5},{5,6},{6,7},{7,8},{8,9},{9,10},{10,1... | collective-permute-start | bytes 1622024 | tf_op jit(solution)/shard_map/ppermute | solution.py:16
  14.0 43.8 %collective-permute-start.3 = (f32[1,192,704]{2,1,0:T(8,128)S(1)}, f32[1,192,704]{2,1,0:T(8,128)S(1)}, u32[]{:S(2)}, u32[]{:S(2)}) collective-permute-start(f32[1,192,704]{2,1,0:T(8,128)S(1)} %get-tuple-element.18), channel_id=1, source_target_pairs={{1,0},{2,1},{3,2},{4,3},{5,4},{6,5},{7,6},{8,7},{9,8},{10,9},{11,1... | collective-permute-start | bytes 1622024 | tf_op jit(solution)/shard_map/ppermute | solution.py:19
  40.7 17.2 %copy-start.12 = (f32[1,192,704]{2,1,0:T(8,128)}, f32[1,192,704]{2,1,0:T(8,128)S(1)}, u32[]{:S(2)}) copy-start(f32[1,192,704]{2,1,0:T(8,128)S(1)} %collective-permute-done.1) | copy-start | bytes 1622020
  57.8 0.8 copy-start.14
  57.8 1.0 copy-start.16
  58.8 0.9 copy-start.1
  60.1 2.8 copy-start.2
  78.7 2.1 copy-start.9
  78.7 2.3 copy-start.13
  80.8 1.1 copy-start.15
  80.8 1.2 copy-start.17
  81.8 1.7 copy-start.18
  82.3 1.3 copy-start.10
  85.0 299.5 %all-reduce.2.cloned.1.call-start = ((), (), s32[]{:S(2)}) async-start(), calls=%async_computation.1 | async-start | bytes 3145728 | tf_op jit(solution)/shard_map/psum | solution.py:92
  85.2 2.7 copy-start.7
  87.9 1.2 copy-start.3
  94.6 1.5 copy-start.11
  95.8 2.3 copy-start.8
  96.2 1.9 copy-start.5
  195.2 1.4 copy-start.6
  197.6 16.6 %collective-permute-start.4 = (f32[192,512]{1,0:T(8,128)}, f32[192,512]{1,0:T(8,128)}, u32[]{:S(2)}, u32[]{:S(2)}) collective-permute-start(f32[192,512]{1,0:T(8,128)} %get-tuple-element.13), channel_id=1, source_target_pairs={{0,240},{16,0},{32,16},{48,32},{64,48},{80,64},{96,80},{112,96},{1... | collective-permute-start | bytes 1179656 | tf_op jit(solution)/shard_map/ppermute | solution.py:27
  203.0 17.0 %collective-permute-start.5 = (f32[192,512]{1,0:T(8,128)}, f32[192,512]{1,0:T(8,128)}, u32[]{:S(2)}, u32[]{:S(2)}) collective-permute-start(f32[192,512]{1,0:T(8,128)} %get-tuple-element.15), channel_id=1, source_target_pairs={{0,15},{1,0},{2,1},{3,2},{4,3},{5,4},{6,5},{7,6},{8,7},{9,8},{10,9... | collective-permute-start | bytes 1179656 | tf_op jit(solution)/shard_map/ppermute | solution.py:27
  203.0 185.4 %slice-start = ((f32[5,192,192]{2,1,0:T(8,128)}), f32[2,192,192]{2,1,0:T(8,128)S(1)}, s32[]{:S(2)}) async-start(f32[5,192,192]{2,1,0:T(8,128)} %copy-done.8), calls=%async_computation.2 | async-start | bytes 786432 | tf_op jit(solution)/shard_map/slice | solution.py:80
  203.0 185.5 %slice-start.1 = ((f32[5,192,192]{2,1,0:T(8,128)}), f32[1,192,192]{2,1,0:T(8,128)S(1)}, s32[]{:S(2)}) async-start(f32[5,192,192]{2,1,0:T(8,128)} %copy-done.8), calls=%async_computation.3 | async-start | bytes 393216 | tf_op jit(solution)/shard_map/slice | solution.py:80
Sparse Core Ops, SparseCore 0:
  85.1 87.0 all-gather.1
  183.2 201.2 all-reduce.1
where the time goes:
time: 403 us; the launch traced here: 399 us
  waiting for transfers between devices  284 us (70%)
  matrix products  63 us (16%)
  starting transfers between devices  19.3 us (5%)
  between operations  14.1 us (3%)
  local copies, waits for them, and re-layouts  12.9 us (3%)
  other arithmetic  5.36 us (1%)
    psum x1, waiting for transfers between devices, per_device(): summed = lax.psum(incomplete_total, 'narrow')  162 us
    all_gather x1, waiting for transfers between devices, per_device(): lax.all_gather(restricted_residual, 'wide', axis=0, tiled=True)  70.4 us
    ppermute x2, waiting for transfers between devices, extended(): lax.ppermute(lax.slice_in_dim(block, block.shape[dim] - width, None, axis...  22 us
    ppermute x2, waiting for transfers between devices, passed_along(): return lax.ppermute(value, axis, pairs)  17 us
    dot_general x12, matrix products, newton_schulz(): jnp.einsum('bij,bjk->bik', matrices, approx, precision=exact_arithmetic_m...  16.5 us
    dot_general x12, matrix products, newton_schulz(): jnp.einsum('bij,bjk->bik', approx, product, precision=exact_arithmetic_mode)  14.3 us
    dot_general x4, matrix products, apply_faces(): jnp.einsum('fij,fjr->fir', blocks, fields, precision=exact_arithmetic_mode)  13.4 us
    ppermute x2, waiting for transfers between devices, extended(): lax.ppermute(lax.slice_in_dim(block, 0, width, axis=dim), axis, backward)  12.8 us
  transfers between devices with their start and end apart: 8, of which 7 were waited for; matrix products, arithmetic and copies ran while one was open for 8% of the time, Pallas kernels for 0%

commit v1 on v0

--- a/solution.py
+++ b/solution.py
@@ -84,7 +84,10 @@
     restricted_residual = restricted_residual.reshape(-1, columns_count)
     incomplete_total = jnp.dot(
         coarse_inverse,
-        lax.all_gather(restricted_residual, "wide", axis=0, tiled=True),
+        jnp.concatenate(
+            lax.all_to_all(jnp.stack([restricted_residual] * lax.axis_size("wide")), "wide", 0, 0),
+            axis=0,
+        ),
         precision=exact_arithmetic_mode,
         preferred_element_type=jnp.float32,
     )

time: 403 us -> 362 us (0.90)
  waiting for transfers between devices: 284 us -> 226 us
  starting transfers between devices: 19.3 us -> 36 us
    all_gather x1 -> x0, waiting for transfers between devices: 70.4 us -> none  [per_device(): lax.all_gather(restricted_residual, 'wide', axis=0, tiled=True)]
    all_to_all x0 -> x1, starting transfers between devices: none -> 19.3 us  [per_device(): lax.all_to_all(jnp.stack([restricted_residual] * lax.axis_size('wide')),...]
    all_to_all x0 -> x1, waiting for transfers between devices: none -> 18.6 us  [per_device(): lax.all_to_all(jnp.stack([restricted_residual] * lax.axis_size('wide')),...]
    psum x1, waiting for transfers between devices: 162 us -> 147 us  [per_device(): summed = lax.psum(incomplete_total, 'narrow')]
    ppermute x2, waiting for transfers between devices: 17 us -> 25.6 us  [passed_along(): return lax.ppermute(value, axis, pairs)]
  transfers between devices with their start and end apart: 8 -> 8, of which waited for: 7 -> 7; matrix products, arithmetic and copies ran while one was open for 8% -> 9% of each run, Pallas kernels for 0% -> 0%
where the time goes in v1:
time: 362 us; the launch traced here: 358 us
  waiting for transfers between devices  226 us (62%)
  matrix products  62.4 us (17%)
  starting transfers between devices  36 us (10%)
  local copies, waits for them, and re-layouts  14.3 us (4%)
  between operations  14.1 us (4%)
  other arithmetic  5.38 us (1%)
    psum x1, waiting for transfers between devices, per_device(): summed = lax.psum(incomplete_total, 'narrow')  147 us
    ppermute x2, waiting for transfers between devices, passed_along(): return lax.ppermute(value, axis, pairs)  25.6 us
    ppermute x2, waiting for transfers between devices, extended(): lax.ppermute(lax.slice_in_dim(block, block.shape[dim] - width, None, axis...  22 us
    all_to_all x1, starting transfers between devices, per_device(): lax.all_to_all(jnp.stack([restricted_residual] * lax.axis_size('wide')),...  19.3 us
    all_to_all x1, waiting for transfers between devices, per_device(): lax.all_to_all(jnp.stack([restricted_residual] * lax.axis_size('wide')),...  18.6 us
    dot_general x12, matrix products, newton_schulz(): jnp.einsum('bij,bjk->bik', matrices, approx, precision=exact_arithmetic_m...  16.5 us
    dot_general x12, matrix products, newton_schulz(): jnp.einsum('bij,bjk->bik', approx, product, precision=exact_arithmetic_mode)  14.3 us
    dot_general x4, matrix products, apply_faces(): jnp.einsum('fij,fjr->fir', blocks, fields, precision=exact_arithmetic_mode)  13.4 us
  transfers between devices with their start and end apart: 8, of which 7 were waited for; matrix products, arithmetic and copies ran while one was open for 9% of the time, Pallas kernels for 0%

profile of v1, /device:TPU:8, one launch (start us, length us, event | category | flops | bytes accessed | tf_op | source)
XLA Modules:
  0.0 358.1 jit_solution(9225243736091412455)
XLA Ops:
  6.5 1.6 slice_bitcast_fusion
  8.8 2.0 collective-permute-start
  10.8 2.8 collective-permute-start.1
  14.0 8.9 %collective-permute-start.3 = (f32[1,192,704]{2,1,0:T(8,128)S(1)}, f32[1,192,704]{2,1,0:T(8,128)S(1)}, u32[]{:S(2)}, u32[]{:S(2)}) collective-permute-start(f32[1,192,704]{2,1,0:T(8,128)S(1)} %get-tuple-element.18), channel_id=1, source_target_pairs={{1,0},{2,1},{3,2},{4,3},{5,4},{6,5},{7,6},{8,7},{9,8},{10,9},{11,1... | collective-permute-start | bytes 1622024 | tf_op jit(solution)/shard_map/ppermute | solution.py:19
  22.9 5.0 %collective-permute-done = f32[1,192,704]{2,1,0:T(8,128)S(1)} collective-permute-done((f32[1,192,704]{2,1,0:T(8,128)S(1)}, f32[1,192,704]{2,1,0:T(8,128)S(1)}, u32[]{:S(2)}, u32[]{:S(2)}) %collective-permute-start) | collective-permute-done | bytes 540704 | tf_op jit(solution)/shard_map/ppermute | solution.py:16
  27.9 12.8 %collective-permute-done.1 = f32[1,192,704]{2,1,0:T(8,128)S(1)} collective-permute-done((f32[1,192,704]{2,1,0:T(8,128)S(1)}, f32[1,192,704]{2,1,0:T(8,128)S(1)}, u32[]{:S(2)}, u32[]{:S(2)}) %collective-permute-start.1) | collective-permute-done | bytes 540704 | tf_op jit(solution)/shard_map/ppermute | solution.py:19
  40.7 17.0 %collective-permute-done.2 = f32[1,192,704]{2,1,0:T(8,128)S(1)} collective-permute-done((f32[1,192,704]{2,1,0:T(8,128)S(1)}, f32[1,192,704]{2,1,0:T(8,128)S(1)}, u32[]{:S(2)}, u32[]{:S(2)}) %collective-permute-start.2) | collective-permute-done | bytes 540704 | tf_op jit(solution)/shard_map/ppermute | solution.py:16
  60.1 2.8 fusion.22
  62.9 1.2 convolution_subtract_fusion.11
  65.2 1.1 convolution_subtract_fusion.10
  66.3 1.1 fusion.46
  67.4 1.1 convolution_subtract_fusion.9
  68.5 1.1 fusion.47
  69.6 1.1 convolution_subtract_fusion.8
  70.8 1.1 fusion.48
  71.8 1.1 convolution_subtract_fusion.7
  73.0 1.3 fusion.49
  74.3 1.1 convolution_subtract_fusion.6
  75.4 1.1 fusion.50
  76.5 1.1 convolution_subtract_fusion.5
  77.6 1.1 fusion.51
  78.7 2.1 convolution_subtract_fusion.4
  82.3 1.3 copy-done.10
  84.3 1.4 stack.43
  85.7 19.3 %all-to-all-start = ((f32[16,48,512]{2,1,0:T(8,128)}), f32[16,48,512]{2,1,0:T(8,128)}, u32[]{:S(2)}, u32[]{:S(2)}) async-start(f32[16,48,512]{2,1,0:T(8,128)} %stack.43), calls=%async_computation | async-start | bytes 3145728 | tf_op jit(solution)/shard_map/all_to_all | solution.py:88
  105.3 2.7 fusion.52
  108.0 1.1 convolution_subtract_fusion.3
  110.2 1.1 convolution_subtract_fusion.2
  111.4 1.1 fusion.54
  112.5 1.1 convolution_subtract_fusion.1
  114.7 1.1 convolution_subtract_fusion
  116.2 1.8 fusion.56
  118.1 3.8 %fusion.5 = bf16[6,512,192]{1,2,0:T(8,128)(2,1)} fusion(f32[1,192,512]{2,1,0:T(8,128)S(1)} %slice.192, f32[5,192,512]{2,1,0:T(8,128)S(1)} %fusion.56, f32[1,1,6,192,192]{4,3,2,1,0:T(8,128)S(1)} %copy-done.5), kind=kOutput, calls=%fused_computation.7 | convolution fusion | flops 1360134144 | bytes 4423680 | tf_op jit(solution)/shard_map/fij,fjr->fir/dot_general | solution.py:42
  121.9 18.6 %all-to-all-done = f32[16,48,512]{2,1,0:T(8,128)} async-done(((f32[16,48,512]{2,1,0:T(8,128)}), f32[16,48,512]{2,1,0:T(8,128)}, u32[]{:S(2)}, u32[]{:S(2)}) %all-to-all-start) | async-done | bytes 1572896 | tf_op jit(solution)/shard_map/all_to_all | solution.py:88
  140.5 10.8 %convolution_bitcast_fusion.2 = f32[768,512]{0,1:T(8,128)} fusion(f32[768,512]{1,0:T(8,128)} %bitcast.29, f32[768,768]{1,0:T(8,128)} %param.9), kind=kOutput, calls=%fused_computation.8 | convolution fusion | flops 3623878656 | bytes 5505024 | tf_op jit(solution)/shard_map/dot_general | solution.py:85
  151.4 4.6 %convolution_bitcast_fusion = f32[1152,512]{0,1:T(8,128)} fusion(bf16[1152,512]{1,0:T(8,128)(2,1)} %bitcast.134, bf16[1,1,1152,1152]{3,2,1,0:T(8,128)(2,1)S(1)} %copy-done), kind=kOutput, calls=%fused_computation | convolution fusion | flops 1358954496 | bytes 6193152 | tf_op jit(solution)/shard_map/dot_general | solution.py:99
  155.9 3.2 copy.9
  159.2 4.4 %convolution_bitcast_fusion.1 = f32[6,192,512]{2,1,0:T(8,128)S(1)} fusion(f32[6,192,512]{2,1,0:T(8,128)} %bitcast.133, f32[1,1,6,192,192]{4,3,2,1,0:T(8,128)} %param.6), kind=kOutput, calls=%fused_computation.6 | convolution fusion | flops 1358954496 | bytes 5603328 | tf_op jit(solution)/shard_map/fij,fjr->fir/dot_general | solution.py:42
  163.5 1.4 copy-done.6
  165.0 1.1 slice_bitcast_fusion.4
  166.0 2.1 collective-permute-start.4
  168.7 18.1 %collective-permute-done.4 = f32[192,512]{1,0:T(8,128)} collective-permute-done((f32[192,512]{1,0:T(8,128)}, f32[192,512]{1,0:T(8,128)}, u32[]{:S(2)}, u32[]{:S(2)}) %collective-permute-start.4) | collective-permute-done | bytes 393248 | tf_op jit(solution)/shard_map/ppermute | solution.py:27
  186.8 7.5 %collective-permute-done.5 = f32[192,512]{1,0:T(8,128)} collective-permute-done((f32[192,512]{1,0:T(8,128)}, f32[192,512]{1,0:T(8,128)}, u32[]{:S(2)}, u32[]{:S(2)}) %collective-permute-start.5) | collective-permute-done | bytes 393248 | tf_op jit(solution)/shard_map/ppermute | solution.py:27
  194.3 2.4 fusion.35
  196.7 146.9 %all-reduce.2.cloned.1.call-done = f32[768,512]{0,1:T(8,128)} async-done(((f32[768,512]{0,1:T(8,128)}), f32[768,512]{0,1:T(8,128)}) %all-reduce.2.cloned.1.call-update) | async-done | bytes 1572880 | tf_op jit(solution)/shard_map/psum | solution.py:95
  343.7 1.2 constant_dynamic-slice_fusion
  345.6 2.0 convolution_bitcast_fusion.3
  347.6 3.5 fusion.8
  (67 shorter events, 10.9 us)
Async XLA Ops:
  6.5 144.8 %copy-start = (bf16[1,1,1152,1152]{3,2,1,0:T(8,128)(2,1)S(1)}, bf16[1,1,1152,1152]{3,2,1,0:T(8,128)(2,1)}, u32[]{:S(2)}) copy-start(bf16[1,1,1152,1152]{3,2,1,0:T(8,128)(2,1)} %param.7) | copy-start | bytes 7962628
  6.5 1.9 copy-start.4
  8.8 19.0 %collective-permute-start = (f32[1,192,704]{2,1,0:T(8,128)S(1)}, f32[1,192,704]{2,1,0:T(8,128)S(1)}, u32[]{:S(2)}, u32[]{:S(2)}) collective-permute-start(f32[1,192,704]{2,1,0:T(8,128)S(1)} %get-tuple-element.23), channel_id=1, source_target_pairs={{0,16},{16,32},{32,48},{48,64},{64,80},{80,96},{96,112},{112,128},... | collective-permute-start | bytes 1622024 | tf_op jit(solution)/shard_map/ppermute | solution.py:16
  10.8 29.9 %collective-permute-start.1 = (f32[1,192,704]{2,1,0:T(8,128)S(1)}, f32[1,192,704]{2,1,0:T(8,128)S(1)}, u32[]{:S(2)}, u32[]{:S(2)}) collective-permute-start(f32[1,192,704]{2,1,0:T(8,128)S(1)} %get-tuple-element.22), channel_id=1, source_target_pairs={{16,0},{32,16},{48,32},{64,48},{80,64},{96,80},{112,96},{128,112},... | collective-permute-start | bytes 1622024 | tf_op jit(solution)/shard_map/ppermute | solution.py:19
  13.9 43.8 %collective-permute-start.2 = (f32[1,192,704]{2,1,0:T(8,128)S(1)}, f32[1,192,704]{2,1,0:T(8,128)S(1)}, u32[]{:S(2)}, u32[]{:S(2)}) collective-permute-start(f32[1,192,704]{2,1,0:T(8,128)S(1)} %get-tuple-element.19), channel_id=1, source_target_pairs={{0,1},{1,2},{2,3},{3,4},{4,5},{5,6},{6,7},{7,8},{8,9},{9,10},{10,1... | collective-permute-start | bytes 1622024 | tf_op jit(solution)/shard_map/ppermute | solution.py:16
  14.0 43.8 %collective-permute-start.3 = (f32[1,192,704]{2,1,0:T(8,128)S(1)}, f32[1,192,704]{2,1,0:T(8,128)S(1)}, u32[]{:S(2)}, u32[]{:S(2)}) collective-permute-start(f32[1,192,704]{2,1,0:T(8,128)S(1)} %get-tuple-element.18), channel_id=1, source_target_pairs={{1,0},{2,1},{3,2},{4,3},{5,4},{6,5},{7,6},{8,7},{9,8},{10,9},{11,1... | collective-permute-start | bytes 1622024 | tf_op jit(solution)/shard_map/ppermute | solution.py:19
  40.7 17.2 %copy-start.12 = (f32[1,192,704]{2,1,0:T(8,128)}, f32[1,192,704]{2,1,0:T(8,128)S(1)}, u32[]{:S(2)}) copy-start(f32[1,192,704]{2,1,0:T(8,128)S(1)} %collective-permute-done.1) | copy-start | bytes 1622020
  57.7 0.9 copy-start.14
  57.8 1.0 copy-start.16
  58.8 0.9 copy-start.1
  60.1 2.8 copy-start.2
  78.7 2.1 copy-start.9
  78.7 2.3 copy-start.13
  80.8 1.1 copy-start.15
  80.8 1.2 copy-start.17
  81.8 1.7 copy-start.18
  82.3 1.3 copy-start.10
  85.7 54.8 %all-to-all-start = ((f32[16,48,512]{2,1,0:T(8,128)}), f32[16,48,512]{2,1,0:T(8,128)}, u32[]{:S(2)}, u32[]{:S(2)}) async-start(f32[16,48,512]{2,1,0:T(8,128)} %stack.43), calls=%async_computation | async-start | bytes 3145728 | tf_op jit(solution)/shard_map/all_to_all | solution.py:88
  105.0 238.7 %all-reduce.2.cloned.1.call-start = ((), (), s32[]{:S(2)}) async-start(), calls=%async_computation.1 | async-start | bytes 3145728 | tf_op jit(solution)/shard_map/psum | solution.py:95
  105.3 2.7 copy-start.7
  107.9 1.2 copy-start.3
  114.7 1.5 copy-start.11
  115.8 2.3 copy-start.8
  116.2 1.9 copy-start.5
  163.5 1.4 copy-start.6
  166.0 20.8 %collective-permute-start.4 = (f32[192,512]{1,0:T(8,128)}, f32[192,512]{1,0:T(8,128)}, u32[]{:S(2)}, u32[]{:S(2)}) collective-permute-start(f32[192,512]{1,0:T(8,128)} %get-tuple-element.13), channel_id=1, source_target_pairs={{0,240},{16,0},{32,16},{48,32},{64,48},{80,64},{96,80},{112,96},{1... | collective-permute-start | bytes 1179656 | tf_op jit(solution)/shard_map/ppermute | solution.py:27
  168.2 26.2 %collective-permute-start.5 = (f32[192,512]{1,0:T(8,128)}, f32[192,512]{1,0:T(8,128)}, u32[]{:S(2)}, u32[]{:S(2)}) collective-permute-start(f32[192,512]{1,0:T(8,128)} %get-tuple-element.15), channel_id=1, source_target_pairs={{0,15},{1,0},{2,1},{3,2},{4,3},{5,4},{6,5},{7,6},{8,7},{9,8},{10,9... | collective-permute-start | bytes 1179656 | tf_op jit(solution)/shard_map/ppermute | solution.py:27
  168.7 178.9 %slice-start = ((f32[5,192,192]{2,1,0:T(8,128)}), f32[2,192,192]{2,1,0:T(8,128)S(1)}, s32[]{:S(2)}) async-start(f32[5,192,192]{2,1,0:T(8,128)} %copy-done.8), calls=%async_computation.2 | async-start | bytes 786432 | tf_op jit(solution)/shard_map/slice | solution.py:80
  168.7 178.9 %slice-start.1 = ((f32[5,192,192]{2,1,0:T(8,128)}), f32[1,192,192]{2,1,0:T(8,128)S(1)}, s32[]{:S(2)}) async-start(f32[5,192,192]{2,1,0:T(8,128)} %copy-done.8), calls=%async_computation.3 | async-start | bytes 393216 | tf_op jit(solution)/shard_map/slice | solution.py:80
Sparse Core Ops, SparseCore 0:
  151.5 192.1 all-reduce.1
